TPU v7x, 32 devices: a whole 2x2x4 slice. The times are simulated.
32 devices in a mesh: brow: 8 (over z, core), bcol: 4 (over y, x).
Axes of the slice: x: 2, y: 2, z: 4, core: 2. Of those that a mesh axis runs over, the one named last changes fastest.
Arguments:
- right_side: float32 [16384, 64], P(('brow', 'bcol')), may hold values from -36 to 36
- tiles: bfloat16 [64, 1, 512, 512], P(('brow', 'bcol')), may hold values from -0.03125 to 0.03125
- row_blocks: int32 [64], P(('brow', 'bcol')), may hold values from 0 to 31, as said below
- col_blocks: int32 [64, 1], P(('brow', 'bcol')), may hold values from 0 to 31, as said below
Outputs:
- solution: float32 [16384, 64], P(('brow', 'bcol'))
- residual: float32 [16384, 64], P(('brow', 'bcol'))
Inputs may be any that keep to these rules, and one draw needn't show every extreme that they name: `row_blocks`: the 2 row blocks of one device lie in different groups, the group of block b being b % 4. `col_blocks`: the tile columns of the device at bcol index j are blocks c with c % 4 == j, different within one row slot.
All inputs are finite; a program needn't handle non-finite values.
Results may differ from a plain program's by a relative error of at most 0.0061.
Values may be sent and summed in bfloat16 or wider, within the bound.
A program may use at most 128 MiB of HBM per device.

v0:
```python
import jax
import jax.numpy as jnp
from jax import lax
from jax.sharding import PartitionSpec as P

ITERS = 3
highest = lax.Precision.HIGHEST


def solve_spd(matrix, rhs):
    factor = jnp.linalg.cholesky(matrix)
    return jax.scipy.linalg.cho_solve((factor, True), rhs)


def gram_of(left, right):
    return jnp.dot(left.T, right, precision=highest)


def right_mult(vectors, coeffs):
    return jnp.einsum("...k,kl->...l", vectors, coeffs, precision=highest)


def shards(right_side, tiles, row_blocks, col_blocks):
    groups = lax.axis_size("bcol")
    gblocks = lax.axis_size("brow")
    tile, width = right_side.shape
    slots, per_row = col_blocks.shape
    flat = tile * width
    slot_group = row_blocks % groups
    slot_place = row_blocks // groups
    col_place = col_blocks // groups
    group_ids = jnp.arange(groups, dtype=jnp.int32)
    block_ids = jnp.arange(gblocks, dtype=jnp.int32)
    matches = slot_group[:, None] == group_ids[None, :]
    wanted = jnp.sum(jnp.where(matches, slot_place[:, None], 0), axis=0)
    active = jnp.any(matches, axis=0).astype(jnp.int32)
    asked = lax.all_to_all(
        jnp.stack([wanted, active], axis=1), "bcol", split_axis=0, concat_axis=0, tiled=True
    )
    send_pick = ((asked[:, 0:1] == block_ids[None, :]) & (asked[:, 1:2] == 1)).astype(jnp.float32)
    slot_pick = matches.astype(jnp.float32)
    col_pick = (col_place.reshape(-1)[:, None] == block_ids[None, :]).astype(jnp.float32)
    own_index = lax.axis_index("brow")
    field = lax.all_gather(right_side[None], "brow", axis=0, tiled=True)

    def own(vectors):
        return lax.dynamic_index_in_dim(vectors, own_index, 0, keepdims=False)

    solution = jnp.zeros_like(field)
    residual = field
    direction = field
    rr_now = lax.psum(gram_of(own(residual), own(residual)), ("brow", "bcol"))
    for step in range(ITERS):
        stacked = direction.astype(jnp.bfloat16).reshape(gblocks, flat)
        outgoing = jnp.dot(
            send_pick.astype(jnp.bfloat16), stacked, preferred_element_type=jnp.float32
        ).astype(jnp.bfloat16)
        arrived = lax.all_to_all(outgoing, "bcol", split_axis=0, concat_axis=0, tiled=True)
        row_dir = jnp.dot(
            slot_pick.astype(jnp.bfloat16), arrived, preferred_element_type=jnp.float32
        )
        row_dir = row_dir.astype(jnp.bfloat16).reshape(slots, tile, width)
        col_dir = jnp.dot(
            col_pick.astype(jnp.bfloat16), stacked, preferred_element_type=jnp.float32
        )
        col_dir = col_dir.astype(jnp.bfloat16).reshape(slots, per_row, tile, width)
        turned = jnp.einsum("scab,sak->scbk", tiles, row_dir, preferred_element_type=jnp.float32)
        direct = jnp.einsum("scab,scbk->sak", tiles, col_dir, preferred_element_type=jnp.float32)
        local = jnp.dot(col_pick.T, turned.reshape(slots * per_row, flat), precision=highest)
        pushing = jnp.dot(slot_pick.T, direct.reshape(slots, flat), precision=highest)
        returned = lax.all_to_all(pushing, "bcol", split_axis=0, concat_axis=0, tiled=True)
        local = local + jnp.dot(send_pick.T, returned, precision=highest)
        summed = lax.psum(local.reshape(gblocks, tile, width), "brow")
        image = 3.0 * direction + summed
        curve = lax.psum(gram_of(own(direction), own(image)), ("brow", "bcol"))
        alpha = solve_spd(curve, rr_now)
        solution = solution + right_mult(direction, alpha)
        residual = residual - right_mult(image, alpha)
        if step + 1 < ITERS:
            fresh = lax.psum(gram_of(own(residual), own(residual)), ("brow", "bcol"))
            beta = solve_spd(rr_now, fresh)
            direction = residual + right_mult(direction, beta)
            rr_now = fresh
    return (own(solution), own(residual))


def solution(mesh):
    placed = (
        P(("brow", "bcol"), None),
        P(("brow", "bcol"), None, None, None),
        P(("brow", "bcol")),
        P(("brow", "bcol"), None),
    )
    return jax.shard_map(
        shards,
        mesh=mesh,
        in_specs=placed,
        out_specs=(P(("brow", "bcol"), None), P(("brow", "bcol"), None)),
        check_vma=False,
    )
```

profile of v0, /device:TPU:0, one launch (start us, length us, event | category | flops | bytes accessed | tf_op | source)
XLA Modules:
  0.0 628.7 jit_solution(16731248828745427380)
XLA Ops:
  9.4 5.2 all-to-all-start
  15.3 3.9 all-to-all-done
  19.4 15.1 %all-gather.3.cloned.1.call-done = f32[4096,64]{0,1:T(8,128)} async-done(((f32[512,64]{0,1:T(8,128)}), f32[4096,64]{0,1:T(8,128)}) %all-gather.3.cloned.1.call-update) | async-done | bytes 1048592 | tf_op jit(solution)/shard_map/all_gather | solution.py:44
  43.1 3.6 all-to-all-start.1
  50.0 2.5 all-to-all-done.1
  52.5 4.1 all-to-all-start.2
  60.2 3.8 all-to-all-done.2
  64.0 2.4 convolution_add_fusion.2
  66.4 2.2 reshape.119
  68.6 3.2 copy.173
  72.3 57.7 %all-reduce.5.cloned.1.call-done = f32[8,512,64]{1,2,0:T(8,128)} async-done(((f32[8,512,64]{1,2,0:T(8,128)}), f32[8,512,64]{1,2,0:T(8,128)}) %all-reduce.5.cloned.1.call-update) | async-done | bytes 1048592 | tf_op jit(solution)/shard_map/psum | solution.py:73
  131.8 40.0 %all-reduce = (f32[64,64]{0,1:T(8,128)S(1)}, f32[64,64]{0,1:T(8,128)S(1)}) all-reduce(f32[64,64]{0,1:T(8,128)S(1)} %fusion.29, f32[64,64]{0,1:T(8,128)S(1)} %fusion.31), channel_id=1, replica_groups=mesh['brow'=8,'bcol'=4] {'brow','bcol'}, use_global_device_ids=true, to_apply=%region_6.8 | all-reduce | flops 8192 | bytes 65536 | tf_op jit(solution)/shard_map/psum | solution.py:52
  171.8 5.8 cholesky.89
  179.0 4.9 custom-call.11
  187.1 40.0 %psum.66 = f32[64,64]{0,1:T(8,128)S(1)} all-reduce(f32[64,64]{0,1:T(8,128)S(1)} %fusion.41), channel_id=1, replica_groups=mesh['brow'=8,'bcol'=4] {'brow','bcol'}, use_global_device_ids=true, to_apply=%region_7.10 | all-reduce | flops 4096 | bytes 32768 | tf_op jit(solution)/shard_map/psum | solution.py:80
  227.1 5.8 cholesky.100
  234.3 4.9 custom-call.12
  239.7 3.1 fusion.102
  242.8 2.4 copy.185
  245.2 2.9 reshape.120
  255.0 4.7 all-to-all-start.3
  261.5 2.1 convolution_bitcast_fusion.7
  270.7 4.2 all-to-all-start.4
  283.7 3.4 convolution_add_fusion.1
  287.1 3.4 reshape.125
  290.5 3.2 copy.192
  293.7 5.8 cholesky.122
  300.9 4.9 custom-call.14
  305.8 46.6 %all-reduce.7.cloned.1.call-done = f32[8,512,64]{1,2,0:T(8,128)} async-done(((f32[8,512,64]{1,2,0:T(8,128)}), f32[8,512,64]{1,2,0:T(8,128)}) %all-reduce.7.cloned.1.call-update) | async-done | bytes 1048592 | tf_op jit(solution)/shard_map/psum | solution.py:73
  355.1 39.8 %psum.68 = f32[64,64]{0,1:T(8,128)S(1)} all-reduce(f32[64,64]{0,1:T(8,128)S(1)} %fusion.38), channel_id=1, replica_groups=mesh['brow'=8,'bcol'=4] {'brow','bcol'}, use_global_device_ids=true, to_apply=%region_9.12 | all-reduce | flops 4096 | bytes 32768 | tf_op jit(solution)/shard_map/psum | solution.py:75
  395.0 5.8 cholesky.111
  402.2 4.9 custom-call.13
  408.2 2.7 convolution_subtract_fusion
  412.2 40.0 %psum.69 = f32[64,64]{1,0:T(8,128)S(1)} all-reduce(f32[64,64]{1,0:T(8,128)S(1)} %fusion.36), channel_id=1, replica_groups=mesh['brow'=8,'bcol'=4] {'brow','bcol'}, use_global_device_ids=true, to_apply=%region_10.13 | all-reduce | flops 4096 | bytes 32768 | tf_op jit(solution)/shard_map/psum | solution.py:80
  452.7 3.6 fusion.103
  456.2 2.4 copy.199
  458.6 2.9 reshape.126
  467.8 4.5 all-to-all-start.5
  473.2 2.1 convolution_bitcast_fusion.5
  482.4 4.2 all-to-all-start.6
  495.5 3.3 convolution_add_fusion
  498.9 3.4 reshape.131
  502.3 3.2 copy.206
  507.5 2.1 fusion.104
  509.6 54.4 %all-reduce.9.cloned.1.call-done = f32[8,512,64]{1,2,0:T(8,128)} async-done(((f32[8,512,64]{1,2,0:T(8,128)}), f32[8,512,64]{1,2,0:T(8,128)}) %all-reduce.9.cloned.1.call-update) | async-done | bytes 1048592 | tf_op jit(solution)/shard_map/psum | solution.py:73
  565.9 39.4 %psum.71 = f32[64,64]{0,1:T(8,128)S(1)} all-reduce(f32[64,64]{0,1:T(8,128)S(1)} %fusion.33), channel_id=1, replica_groups=mesh['brow'=8,'bcol'=4] {'brow','bcol'}, use_global_device_ids=true, to_apply=%region_12.15 | all-reduce | flops 4096 | bytes 32768 | tf_op jit(solution)/shard_map/psum | solution.py:75
  605.4 5.8 cholesky.133
  612.6 4.9 custom-call.15
  (153 shorter events, 92.8 us)
Async XLA Ops:
  7.2 39.7 %copy-start = (bf16[2,1,512,512]{3,2,1,0:T(8,128)(2,1)S(1)}, bf16[2,1,512,512]{3,2,1,0:T(8,128)(2,1)}, u32[]{:S(2)}) copy-start(bf16[2,1,512,512]{3,2,1,0:T(8,128)(2,1)} %param.8) | copy-start | bytes 3145732
  7.2 27.3 %all-gather.3.cloned.1.call-start = ((), (), s32[]{:S(2)}) async-start(), calls=%async_computation.10 | async-start | bytes 1179648 | tf_op jit(solution)/shard_map/all_gather | solution.py:44
  9.4 9.7 %all-to-all-start = ((s32[4,1,2]{2,1,0:T(1,128)}), s32[4,1,2]{2,1,0:T(1,128)S(1)}, u32[]{:S(2)}, u32[]{:S(2)}) async-start(s32[4,1,2]{2,1,0:T(1,128)} %copy.164), calls=%async_computation | async-start | bytes 4096 | tf_op jit(solution)/shard_map/all_to_all | solution.py:37
  43.1 9.4 %all-to-all-start.1 = ((bf16[4,2,16384]{2,1,0:T(2,128)(2,1)}), bf16[4,2,16384]{2,1,0:T(2,128)(2,1)S(1)}, u32[]{:S(2)}, u32[]{:S(2)}) async-start(bf16[4,2,16384]{2,1,0:T(2,128)(2,1)} %reshape.142), calls=%async_computation.1 | async-start | bytes 524288 | tf_op jit(solution)/shard_map/all_to_all | solution.py:58
  52.5 11.6 %all-to-all-start.2 = ((f32[4,1,32768]{2,1,0:T(1,128)}), f32[4,1,32768]{2,1,0:T(1,128)}, u32[]{:S(2)}, u32[]{:S(2)}) async-start(f32[4,1,32768]{2,1,0:T(1,128)} %copy.172), calls=%async_computation.2 | async-start | bytes 1048576 | tf_op jit(solution)/shard_map/all_to_all | solution.py:71
  56.6 73.3 %all-reduce.5.cloned.1.call-start = ((), (), s32[]{:S(2)}) async-start(), calls=%async_computation.7 | async-start | bytes 2097152 | tf_op jit(solution)/shard_map/psum | solution.py:73
  68.6 61.3 %copy-start.1 = (f32[4096,64]{0,1:T(8,128)S(1)}, f32[4096,64]{0,1:T(8,128)}, u32[]{:S(2)}) copy-start(f32[4096,64]{0,1:T(8,128)} %all-gather.3.cloned.1.call-done) | copy-start | bytes 3145732
  129.9 54.6 %copy-start.6 = (f32[8,512,64]{1,2,0:T(8,128)S(1)}, f32[8,512,64]{1,2,0:T(8,128)}, u32[]{:S(2)}) copy-start(f32[8,512,64]{1,2,0:T(8,128)} %all-reduce.5.cloned.1.call-done) | copy-start | bytes 3145732
  184.5 1.3 copy-start.7
  185.8 1.0 copy-start.2
  255.0 15.7 %all-to-all-start.3 = ((bf16[4,2,16384]{2,1,0:T(2,128)(2,1)}), bf16[4,2,16384]{2,1,0:T(2,128)(2,1)S(1)}, u32[]{:S(2)}, u32[]{:S(2)}) async-start(bf16[4,2,16384]{2,1,0:T(2,128)(2,1)} %reshape.144), calls=%async_computation.3 | async-start | bytes 524288 | tf_op jit(solution)/shard_map/all_to_all | solution.py:58
  270.7 13.0 %all-to-all-start.4 = ((f32[4,1,32768]{2,1,0:T(1,128)}), f32[4,1,32768]{2,1,0:T(1,128)}, u32[]{:S(2)}, u32[]{:S(2)}) async-start(f32[4,1,32768]{2,1,0:T(1,128)} %copy.191), calls=%async_computation.4 | async-start | bytes 1048576 | tf_op jit(solution)/shard_map/all_to_all | solution.py:71
  274.9 77.4 %all-reduce.7.cloned.1.call-start = ((), (), s32[]{:S(2)}) async-start(), calls=%async_computation.8 | async-start | bytes 2097152 | tf_op jit(solution)/shard_map/psum | solution.py:73
  353.8 1.0 copy-start.5
  407.6 0.6 copy-start.9
  410.9 1.0 copy-start.4
  452.2 6.4 %copy-start.11 = (f32[64,64]{1,0:T(8,128)}, f32[64,64]{1,0:T(8,128)S(1)}, u32[]{:S(2)}) copy-start(f32[64,64]{1,0:T(8,128)S(1)} %psum.69) | copy-start | bytes 49156
  467.8 14.5 %all-to-all-start.5 = ((bf16[4,2,16384]{2,1,0:T(2,128)(2,1)}), bf16[4,2,16384]{2,1,0:T(2,128)(2,1)S(1)}, u32[]{:S(2)}, u32[]{:S(2)}) async-start(bf16[4,2,16384]{2,1,0:T(2,128)(2,1)} %reshape.146), calls=%async_computation.5 | async-start | bytes 524288 | tf_op jit(solution)/shard_map/all_to_all | solution.py:58
  482.4 13.2 %all-to-all-start.6 = ((f32[4,1,32768]{2,1,0:T(1,128)}), f32[4,1,32768]{2,1,0:T(1,128)}, u32[]{:S(2)}, u32[]{:S(2)}) async-start(f32[4,1,32768]{2,1,0:T(1,128)} %copy.205), calls=%async_computation.6 | async-start | bytes 1048576 | tf_op jit(solution)/shard_map/all_to_all | solution.py:71
  486.6 77.5 %all-reduce.9.cloned.1.call-start = ((), (), s32[]{:S(2)}) async-start(), calls=%async_computation.9 | async-start | bytes 2097152 | tf_op jit(solution)/shard_map/psum | solution.py:73
  502.3 3.2 copy-start.8
  505.4 2.1 copy-start.10
  507.5 56.6 %copy-start.3 = (f32[8,512,64]{1,2,0:T(8,128)S(1)}, f32[8,512,64]{1,2,0:T(8,128)}, u32[]{:S(2)}) copy-start(f32[8,512,64]{1,2,0:T(8,128)} %get-tuple-element.11) | copy-start | bytes 3145732
  509.6 107.9 %copy-start.12 = (f32[64,64]{1,0:T(8,128)S(1)}, f32[64,64]{1,0:T(8,128)}, u32[]{:S(2)}) copy-start(f32[64,64]{1,0:T(8,128)} %copy-done.11) | copy-start | bytes 49156
Sparse Core Ops, SparseCore 0:
  9.6 24.7 all-gather.2
  72.0 57.8 all-reduce.4
  293.8 58.5 all-reduce.6
  505.6 58.4 all-reduce.8
where the time goes:
time: 639 us; the launch traced here: 629 us
  blocking collectives  199 us (31%)
  waiting for transfers between devices  185 us (29%)
  other arithmetic  73 us (11%)
  local copies, waits for them, and re-layouts  67.7 us (11%)
  matrix products  58.6 us (9%)
  starting transfers between devices  30.7 us (5%)
  between operations  14.6 us (2%)
    psum x3, waiting for transfers between devices, shards(): summed = lax.psum(local.reshape(gblocks, tile, width), 'brow')  159 us
    psum x2, blocking collectives, shards(): fresh = lax.psum(gram_of(own(residual), own(residual)), ('brow', 'bcol'))  80 us
    psum x2, blocking collectives, shards(): curve = lax.psum(gram_of(own(direction), own(image)), ('brow', 'bcol'))  79.3 us
    psum x1, blocking collectives, shards(): rr_now = lax.psum(gram_of(own(residual), own(residual)), ('brow', 'bcol'))  40 us
    another operation x15, other arithmetic, solve_spd(): factor = jnp.linalg.cholesky(matrix)  32.6 us
    another operation x10, other arithmetic, solve_spd(): return jax.scipy.linalg.cho_solve((factor, True), rhs)  27.7 us
    reshape x6, local copies, waits for them, and re-layouts, shards(): summed = lax.psum(local.reshape(gblocks, tile, width), 'brow')  18.6 us
    dot_general x8, matrix products, right_mult(): return jnp.einsum('...k,kl->...l', vectors, coeffs, precision=highest)  17 us
  transfers between devices with their start and end apart: 11, of which 7 were waited for; matrix products, arithmetic and copies ran while one was open for 10% of the time, Pallas kernels for 0%

commit v1 on v0

--- a/solution.py
+++ b/solution.py
@@ -77,7 +77,9 @@
         solution = solution + right_mult(direction, alpha)
         residual = residual - right_mult(image, alpha)
         if step + 1 < ITERS:
-            fresh = lax.psum(gram_of(own(residual), own(residual)), ("brow", "bcol"))
+            fresh = jnp.sum(
+                lax.all_gather(gram_of(own(residual), own(residual)), ("brow", "bcol")), axis=0
+            )
             beta = solve_spd(rr_now, fresh)
             direction = residual + right_mult(direction, beta)
             rr_now = fresh

time: 639 us -> 716 us (1.12)
  blocking collectives: 199 us -> 268 us
  starting transfers between devices: 30.7 us -> 40.2 us
    all_gather x0 -> x2, blocking collectives: none -> 149 us  [shards(): lax.all_gather(gram_of(own(residual), own(residual)), ('brow', 'bcol'))]
    psum x2 -> x0, blocking collectives: 80 us -> none  [shards(): fresh = lax.psum(gram_of(own(residual), own(residual)), ('brow', 'bcol'))]
    psum x3, starting transfers between devices: 0.21 us -> 12.1 us  [shards(): summed = lax.psum(local.reshape(gblocks, tile, width), 'brow')]
  transfers between devices with their start and end apart: 11 -> 11, of which waited for: 7 -> 7; matrix products, arithmetic and copies ran while one was open for 10% -> 9% of each run, Pallas kernels for 0% -> 0%
where the time goes in v1:
time: 716 us; the launch traced here: 705 us
  blocking collectives  268 us (37%)
  waiting for transfers between devices  183 us (26%)
  other arithmetic  74.4 us (10%)
  local copies, waits for them, and re-layouts  67.1 us (9%)
  matrix products  58.5 us (8%)
  starting transfers between devices  40.2 us (6%)
  between operations  14.8 us (2%)
    psum x3, waiting for transfers between devices, shards(): summed = lax.psum(local.reshape(gblocks, tile, width), 'brow')  157 us
    all_gather x2, blocking collectives, shards(): lax.all_gather(gram_of(own(residual), own(residual)), ('brow', 'bcol'))  149 us
    psum x2, blocking collectives, shards(): curve = lax.psum(gram_of(own(direction), own(image)), ('brow', 'bcol'))  78.9 us
    psum x1, blocking collectives, shards(): rr_now = lax.psum(gram_of(own(residual), own(residual)), ('brow', 'bcol'))  40 us
    another operation x15, other arithmetic, solve_spd(): factor = jnp.linalg.cholesky(matrix)  32.6 us
    another operation x10, other arithmetic, solve_spd(): return jax.scipy.linalg.cho_solve((factor, True), rhs)  27.7 us
    reshape x6, local copies, waits for them, and re-layouts, shards(): summed = lax.psum(local.reshape(gblocks, tile, width), 'brow')  18.6 us
    dot_general x8, matrix products, right_mult(): return jnp.einsum('...k,kl->...l', vectors, coeffs, precision=highest)  17 us
  transfers between devices with their start and end apart: 11, of which 7 were waited for; matrix products, arithmetic and copies ran while one was open for 9% of the time, Pallas kernels for 0%

profile of v1, /device:TPU:0, one launch (start us, length us, event | category | flops | bytes accessed | tf_op | source)
XLA Modules:
  0.0 705.3 jit_solution(593504096018416025)
XLA Ops:
  9.4 5.2 all-to-all-start
  15.3 3.9 all-to-all-done
  19.4 15.1 %all-gather.5.cloned.1.call-done = f32[4096,64]{0,1:T(8,128)} async-done(((f32[512,64]{0,1:T(8,128)}), f32[4096,64]{0,1:T(8,128)}) %all-gather.5.cloned.1.call-update) | async-done | bytes 1048592 | tf_op jit(solution)/shard_map/all_gather | solution.py:44
  43.1 3.6 all-to-all-start.1
  50.0 2.5 all-to-all-done.1
  52.5 4.1 all-to-all-start.2
  60.2 3.8 all-to-all-done.2
  64.0 2.4 convolution_add_fusion.2
  66.4 2.2 reshape.119
  68.6 3.2 copy.169
  72.3 57.7 %all-reduce.5.cloned.1.call-done = f32[8,512,64]{1,2,0:T(8,128)} async-done(((f32[8,512,64]{1,2,0:T(8,128)}), f32[8,512,64]{1,2,0:T(8,128)}) %all-reduce.5.cloned.1.call-update) | async-done | bytes 1048592 | tf_op jit(solution)/shard_map/psum | solution.py:73
  131.8 40.0 %all-reduce = (f32[64,64]{0,1:T(8,128)S(1)}, f32[64,64]{0,1:T(8,128)S(1)}) all-reduce(f32[64,64]{0,1:T(8,128)S(1)} %fusion.29, f32[64,64]{0,1:T(8,128)S(1)} %fusion.31), channel_id=1, replica_groups=mesh['brow'=8,'bcol'=4] {'brow','bcol'}, use_global_device_ids=true, to_apply=%region_6.8 | all-reduce | flops 8192 | bytes 65536 | tf_op jit(solution)/shard_map/psum | solution.py:52
  171.9 5.8 cholesky.89
  179.1 4.9 custom-call.11
  187.2 5.8 cholesky.100
  194.4 4.9 custom-call.12
  199.3 72.1 %all-gather.1 = f32[2048,64]{1,0:T(8,128)S(1)} all-gather(f32[64,64]{1,0:T(8,128)S(1)} %fusion.41), channel_id=3, replica_groups=mesh['brow'=8,'bcol'=4] {'brow','bcol'}, dimensions={0}, use_global_device_ids=true | all-gather | bytes 540672 | tf_op jit(solution)/shard_map/all_gather | solution.py:81
  271.9 3.1 fusion.102
  275.0 2.4 copy.180
  277.4 2.9 reshape.120
  287.2 3.4 all-to-all-start.3
  292.4 2.1 convolution_bitcast_fusion.7
  301.6 4.2 all-to-all-start.4
  305.8 11.8 %all-reduce.7.cloned.1.call-start = ((), (), s32[]{:S(2)}) async-start(), calls=%async_computation.8 | async-start | bytes 2097152 | tf_op jit(solution)/shard_map/psum | solution.py:73
  326.4 3.4 convolution_add_fusion.1
  329.8 3.4 reshape.125
  333.2 3.2 copy.187
  336.4 5.8 cholesky.122
  343.6 4.9 custom-call.14
  348.5 45.5 %all-reduce.7.cloned.1.call-done = f32[8,512,64]{1,2,0:T(8,128)} async-done(((f32[8,512,64]{1,2,0:T(8,128)}), f32[8,512,64]{1,2,0:T(8,128)}) %all-reduce.7.cloned.1.call-update) | async-done | bytes 1048592 | tf_op jit(solution)/shard_map/psum | solution.py:73
  396.7 39.4 %psum.53 = f32[64,64]{0,1:T(8,128)S(1)} all-reduce(f32[64,64]{0,1:T(8,128)S(1)} %fusion.38), channel_id=1, replica_groups=mesh['brow'=8,'bcol'=4] {'brow','bcol'}, use_global_device_ids=true, to_apply=%region_9.12 | all-reduce | flops 4096 | bytes 32768 | tf_op jit(solution)/shard_map/psum | solution.py:75
  436.2 5.8 cholesky.111
  443.4 4.9 custom-call.13
  448.8 2.7 convolution_subtract_fusion
  452.8 76.6 %all-gather.2 = f32[2048,64]{1,0:T(8,128)} all-gather(f32[64,64]{1,0:T(8,128)S(1)} %fusion.36), channel_id=4, replica_groups=mesh['brow'=8,'bcol'=4] {'brow','bcol'}, dimensions={0}, use_global_device_ids=true | all-gather | bytes 540672 | tf_op jit(solution)/shard_map/all_gather | solution.py:81
  531.2 3.6 fusion.103
  534.8 2.4 copy.194
  537.1 2.9 reshape.126
  546.3 3.4 all-to-all-start.5
  559.8 4.2 all-to-all-start.6
  573.0 3.3 convolution_add_fusion
  576.3 3.4 reshape.131
  579.7 3.2 copy.201
  585.0 2.1 fusion.104
  587.1 53.4 %all-reduce.9.cloned.1.call-done = f32[8,512,64]{1,2,0:T(8,128)} async-done(((f32[8,512,64]{1,2,0:T(8,128)}), f32[8,512,64]{1,2,0:T(8,128)}) %all-reduce.9.cloned.1.call-update) | async-done | bytes 1048592 | tf_op jit(solution)/shard_map/psum | solution.py:73
  642.3 39.4 %psum.55 = f32[64,64]{0,1:T(8,128)S(1)} all-reduce(f32[64,64]{0,1:T(8,128)S(1)} %fusion.33), channel_id=1, replica_groups=mesh['brow'=8,'bcol'=4] {'brow','bcol'}, use_global_device_ids=true, to_apply=%region_12.15 | all-reduce | flops 4096 | bytes 32768 | tf_op jit(solution)/shard_map/psum | solution.py:75
  681.9 5.8 cholesky.133
  689.0 4.9 custom-call.15
  (155 shorter events, 95.7 us)
Async XLA Ops:
  7.2 39.7 %copy-start = (bf16[2,1,512,512]{3,2,1,0:T(8,128)(2,1)S(1)}, bf16[2,1,512,512]{3,2,1,0:T(8,128)(2,1)}, u32[]{:S(2)}) copy-start(bf16[2,1,512,512]{3,2,1,0:T(8,128)(2,1)} %param.8) | copy-start | bytes 3145732
  7.2 27.3 %all-gather.5.cloned.1.call-start = ((), (), s32[]{:S(2)}) async-start(), calls=%async_computation.10 | async-start | bytes 1179648 | tf_op jit(solution)/shard_map/all_gather | solution.py:44
  9.4 9.7 %all-to-all-start = ((s32[4,1,2]{2,1,0:T(1,128)}), s32[4,1,2]{2,1,0:T(1,128)S(1)}, u32[]{:S(2)}, u32[]{:S(2)}) async-start(s32[4,1,2]{2,1,0:T(1,128)} %copy.160), calls=%async_computation | async-start | bytes 4096 | tf_op jit(solution)/shard_map/all_to_all | solution.py:37
  43.1 9.4 %all-to-all-start.1 = ((bf16[4,2,16384]{2,1,0:T(2,128)(2,1)}), bf16[4,2,16384]{2,1,0:T(2,128)(2,1)S(1)}, u32[]{:S(2)}, u32[]{:S(2)}) async-start(bf16[4,2,16384]{2,1,0:T(2,128)(2,1)} %reshape.144), calls=%async_computation.1 | async-start | bytes 524288 | tf_op jit(solution)/shard_map/all_to_all | solution.py:58
  52.5 11.6 %all-to-all-start.2 = ((f32[4,1,32768]{2,1,0:T(1,128)}), f32[4,1,32768]{2,1,0:T(1,128)}, u32[]{:S(2)}, u32[]{:S(2)}) async-start(f32[4,1,32768]{2,1,0:T(1,128)} %copy.168), calls=%async_computation.2 | async-start | bytes 1048576 | tf_op jit(solution)/shard_map/all_to_all | solution.py:71
  56.6 73.3 %all-reduce.5.cloned.1.call-start = ((), (), s32[]{:S(2)}) async-start(), calls=%async_computation.7 | async-start | bytes 2097152 | tf_op jit(solution)/shard_map/psum | solution.py:73
  68.6 61.3 %copy-start.1 = (f32[4096,64]{0,1:T(8,128)S(1)}, f32[4096,64]{0,1:T(8,128)}, u32[]{:S(2)}) copy-start(f32[4096,64]{0,1:T(8,128)} %all-gather.5.cloned.1.call-done) | copy-start | bytes 3145732
  129.9 54.6 %copy-start.6 = (f32[8,512,64]{1,2,0:T(8,128)S(1)}, f32[8,512,64]{1,2,0:T(8,128)}, u32[]{:S(2)}) copy-start(f32[8,512,64]{1,2,0:T(8,128)} %all-reduce.5.cloned.1.call-done) | copy-start | bytes 3145732
  184.6 2.6 copy-start.7
  185.9 1.0 copy-start.2
  287.2 14.4 %all-to-all-start.3 = ((bf16[4,2,16384]{2,1,0:T(2,128)(2,1)}), bf16[4,2,16384]{2,1,0:T(2,128)(2,1)S(1)}, u32[]{:S(2)}, u32[]{:S(2)}) async-start(bf16[4,2,16384]{2,1,0:T(2,128)(2,1)} %reshape.146), calls=%async_computation.3 | async-start | bytes 524288 | tf_op jit(solution)/shard_map/all_to_all | solution.py:58
  301.6 24.8 %all-to-all-start.4 = ((f32[4,1,32768]{2,1,0:T(1,128)}), f32[4,1,32768]{2,1,0:T(1,128)}, u32[]{:S(2)}, u32[]{:S(2)}) async-start(f32[4,1,32768]{2,1,0:T(1,128)} %copy.186), calls=%async_computation.4 | async-start | bytes 1048576 | tf_op jit(solution)/shard_map/all_to_all | solution.py:71
  305.8 88.2 %all-reduce.7.cloned.1.call-start = ((), (), s32[]{:S(2)}) async-start(), calls=%async_computation.8 | async-start | bytes 2097152 | tf_op jit(solution)/shard_map/psum | solution.py:73
  395.4 1.0 copy-start.5
  448.8 80.6 %copy-start.9 = (f32[64,64,1]{0,1,2:T(8,128)}, f32[64,64,1]{0,1,2:T(8,128)S(1)}, u32[]{:S(2)}) copy-start(f32[64,64,1]{0,1,2:T(8,128)S(1)} %convolution_bitcast_fusion.13) | copy-start | bytes 49156
  451.5 1.0 copy-start.4
  530.7 6.4 copy-start.11
  546.3 13.5 %all-to-all-start.5 = ((bf16[4,2,16384]{2,1,0:T(2,128)(2,1)}), bf16[4,2,16384]{2,1,0:T(2,128)(2,1)S(1)}, u32[]{:S(2)}, u32[]{:S(2)}) async-start(bf16[4,2,16384]{2,1,0:T(2,128)(2,1)} %reshape.148), calls=%async_computation.5 | async-start | bytes 524288 | tf_op jit(solution)/shard_map/all_to_all | solution.py:58
  559.8 13.2 %all-to-all-start.6 = ((f32[4,1,32768]{2,1,0:T(1,128)}), f32[4,1,32768]{2,1,0:T(1,128)}, u32[]{:S(2)}, u32[]{:S(2)}) async-start(f32[4,1,32768]{2,1,0:T(1,128)} %copy.200), calls=%async_computation.6 | async-start | bytes 1048576 | tf_op jit(solution)/shard_map/all_to_all | solution.py:71
  564.0 76.6 %all-reduce.9.cloned.1.call-start = ((), (), s32[]{:S(2)}) async-start(), calls=%async_computation.9 | async-start | bytes 2097152 | tf_op jit(solution)/shard_map/psum | solution.py:73
  579.7 3.2 copy-start.8
  582.9 2.1 copy-start.10
  585.0 55.6 %copy-start.3 = (f32[8,512,64]{1,2,0:T(8,128)S(1)}, f32[8,512,64]{1,2,0:T(8,128)}, u32[]{:S(2)}) copy-start(f32[8,512,64]{1,2,0:T(8,128)} %get-tuple-element.11) | copy-start | bytes 3145732
  587.1 106.9 %copy-start.12 = (f32[64,64]{1,0:T(8,128)S(1)}, f32[64,64]{1,0:T(8,128)}, u32[]{:S(2)}) copy-start(f32[64,64]{1,0:T(8,128)} %copy-done.11) | copy-start | bytes 49156
Sparse Core Ops, SparseCore 0:
  9.6 24.7 all-gather.4
  72.0 57.8 all-reduce.4
  336.5 57.4 all-reduce.6
  583.0 57.4 all-reduce.8
